TPU v7x, 256 devices: a whole 4x4x8 slice. The times are simulated.
256 devices in a mesh: section: 2 (over core), dp: 16 (over x, y), tensor: 8 (over z).
Axes of the slice: x: 4, y: 4, z: 8, core: 2. Of those that a mesh axis runs over, the one named last changes fastest.
Arguments:
- hidden_states: bfloat16 [2, 4096, 8192], P('section', 'dp', 'tensor'), may hold values from -6 to 6
- base_weight: bfloat16 [2, 8192, 8192], P('section', 'tensor', 'dp'), may hold values from -0.0625 to 0.0625
- shrink_weight: bfloat16 [2, 1024, 16, 8192], P('section', 'dp', None, 'tensor'), may hold values from -0.0625 to 0.0625
- expand_weight: bfloat16 [2, 1024, 16, 8192], P('section', 'dp', None, 'tensor'), may hold values from -1.5 to 1.5
- owner_ids: int32 [2, 4096, 1], P('section', 'dp'), may hold values from 0 to 15; in each aligned block of 256 rows (0 to 255, 256 to 511, ..., all dimensions but the last counted through in order) at most 32 rows name the same one
- adapter_slots: int32 [2, 4096], P('section', 'dp'), may hold values from 0 to 63
Outputs:
- carried: bfloat16 [2, 4096, 8192], P('section', 'dp', 'tensor')
Inputs may be any that keep to these rules, and one draw needn't show every extreme that they name: `owner_ids`: within each aligned block of 256 rows (the rows of one device), no owner is named by more than 32 rows, and one owner is named by exactly 32 rows in some block.
All inputs are finite; a program needn't handle non-finite values.
Results may differ from a plain program's by a relative error of at most 0.017.
Values may be sent and summed in bfloat16 or wider, within the bound.
A program may use at most 128 MiB of HBM per device.

v0:
```python
import jax
import jax.numpy as jnp
from jax import lax
from jax.sharding import PartitionSpec as P


def shifted(array, axis, by):
    count = lax.axis_size(axis)
    return lax.ppermute(array, axis, [(i, (i + by) % count) for i in range(count)])


def local(hidden_states, base_weight, shrink_weight, expand_weight, owner_ids, adapter_slots):
    local_rows = hidden_states[0]
    local_weight = base_weight[0]
    row_count = local_rows.shape[0]
    feature_width = local_rows.shape[1]
    owner_count = lax.axis_size("dp")
    capacity = 2 * row_count // owner_count
    local_count = shrink_weight.shape[1]
    rank_size = shrink_weight.shape[2]
    shrink_table = shrink_weight[0].reshape(local_count * rank_size, feature_width)
    expand_table = expand_weight[0].reshape(local_count * rank_size, feature_width)
    owner_row = owner_ids[0, :, 0]
    slot_row = adapter_slots[0]
    owner_hits = (owner_row[:, None] == jnp.arange(owner_count, dtype=jnp.int32)[None, :]).astype(
        jnp.int32
    )
    arrival = jnp.sum((jnp.cumsum(owner_hits, axis=0) - 1) * owner_hits, axis=1)
    position = owner_row * capacity + arrival
    send_rows = (
        jnp.zeros((owner_count * capacity, feature_width), jnp.bfloat16)
        .at[position]
        .set(local_rows)
    )
    send_ids = jnp.full((owner_count * capacity,), -1, jnp.int32).at[position].set(slot_row)
    send_rows = send_rows.reshape(owner_count, capacity, feature_width)
    send_ids = send_ids.reshape(owner_count, capacity)
    rows_in = lax.all_to_all(send_rows, "dp", split_axis=0, concat_axis=0, tiled=True)
    ids_in = lax.all_to_all(send_ids, "dp", split_axis=0, concat_axis=0, tiled=True)
    flat_rows = rows_in.reshape(-1, feature_width)
    flat_ids = ids_in.reshape(-1)
    slot_total = flat_rows.shape[0]
    onehot = (flat_ids[:, None] == jnp.arange(local_count, dtype=jnp.int32)[None, :]).astype(
        jnp.float32
    )
    projected = lax.dot_general(
        flat_rows, shrink_table, (((1,), (1,)), ((), ())), preferred_element_type=jnp.float32
    )
    partial_value = jnp.einsum(
        "skr,sk->rs", projected.reshape(slot_total, local_count, rank_size), onehot
    )
    summed = lax.psum(partial_value.astype(jnp.bfloat16), "tensor").astype(jnp.float32)
    shrunk = summed.T.astype(jnp.bfloat16)
    spread = (onehot.astype(jnp.bfloat16)[:, :, None] * shrunk[:, None, :]).reshape(
        slot_total, local_count * rank_size
    )
    low_rank = jnp.dot(spread, expand_table, preferred_element_type=jnp.float32).astype(
        jnp.bfloat16
    )
    returned = lax.all_to_all(
        low_rank.reshape(rows_in.shape), "dp", split_axis=0, concat_axis=0, tiled=True
    )
    adapter_rows = returned.reshape(owner_count * capacity, feature_width)[position]
    partial_term = jnp.dot(
        local_rows,
        lax.all_gather(local_weight, "dp", axis=1, tiled=True),
        preferred_element_type=jnp.float32,
    )
    base_term = lax.psum_scatter(
        partial_term.astype(jnp.bfloat16), "tensor", scatter_dimension=1, tiled=True
    ).astype(jnp.float32)
    layer_output = (
        local_rows.astype(jnp.float32) + base_term + adapter_rows.astype(jnp.float32)
    ).astype(jnp.bfloat16)
    carried = shifted(layer_output, "section", 1)
    return carried[None]


def solution(mesh):
    return jax.shard_map(
        local,
        mesh=mesh,
        in_specs=(
            P("section", "dp", "tensor"),
            P("section", "tensor", "dp"),
            P("section", "dp", None, "tensor"),
            P("section", "dp", None, "tensor"),
            P("section", "dp", None),
            P("section", "dp"),
        ),
        out_specs=P("section", "dp", "tensor"),
        check_vma=False,
    )
```

profile of v0, /device:TPU:1, one launch (start us, length us, event | category | flops | bytes accessed | tf_op | source)
XLA Modules:
  0.0 253.4 jit_solution(802769703096249874)
XLA Ops:
  6.5 0.0 copy-start
  6.5 0.0 all-gather.3.cloned.1.call-start
  6.5 0.7 all-gather.3.cloned.1.call-update
  7.3 0.0 reduce-scatter.2.cloned.1.call-start
  7.3 131.5 %all-gather.3.cloned.1.call-done = bf16[1,1024,8192]{2,1,0:T(8,128)(2,1)} async-done(((bf16[1,1024,512]{2,1,0:T(8,128)(2,1)}), bf16[1,1024,8192]{2,1,0:T(8,128)(2,1)}) %all-gather.3.cloned.1.call-update) | async-done | bytes 16777232 | tf_op jit(solution)/shard_map/all_gather | solution.py:66
  138.8 12.4 %fusion.2 = bf16[256,8192]{1,0:T(8,128)(2,1)} fusion(bf16[1,1024,8192]{2,1,0:T(8,128)(2,1)} %all-gather.3.cloned.1.call-done, bf16[1,256,1024]{2,1,0:T(8,128)(2,1)} %param.6), kind=kOutput, calls=%fused_computation.5 | convolution fusion | flops 4297064448 | bytes 21495808 | tf_op jit(solution)/shard_map/dot_general | solution.py:64
  151.2 0.0 reduce-scatter.2.cloned.1.call-update
  151.2 0.7 copy-done.2
  151.8 0.6 reduce-window.6
  152.4 0.2 slice_reduce_fusion
  152.6 0.1 fusion.16
  152.7 1.6 scatter_custom_fusion
  154.3 0.7 all_to_all.12
  155.0 4.7 %all-to-all-start = ((s32[16,1,32]{2,1,0:T(1,128)}), s32[16,1,32]{2,1,0:T(1,128)S(1)}, u32[]{:S(2)}, u32[]{:S(2)}) async-start(s32[16,1,32]{2,1,0:T(1,128)} %all_to_all.12), calls=%async_computation.1 | async-start | bytes 16384 | tf_op jit(solution)/shard_map/all_to_all | solution.py:39
  159.7 2.7 %scatter_custom_fusion.1 = bf16[512,1024]{1,0:T(8,128)(2,1)} fusion(s32[256]{0:T(256)S(1)} %bitcast.59, bf16[1,256,1024]{2,1,0:T(8,128)(2,1)S(1)} %copy-done.1, bf16[]{:T(256)} %constant.16.clone.1), kind=kCustom, calls=%fused_computation.11 | custom fusion | bytes 1572866 | tf_op jit(solution)/shard_map/scatter | solution.py:33
  162.4 3.7 %all-to-all-done = s32[16,1,32]{2,1,0:T(1,128)S(1)} async-done(((s32[16,1,32]{2,1,0:T(1,128)}), s32[16,1,32]{2,1,0:T(1,128)S(1)}, u32[]{:S(2)}, u32[]{:S(2)}) %all-to-all-start) | async-done | bytes 2080 | tf_op jit(solution)/shard_map/all_to_all | solution.py:39
  166.0 3.7 %all-to-all-start.1 = ((bf16[16,32,1024]{2,1,0:T(8,128)(2,1)}), bf16[16,32,1024]{2,1,0:T(8,128)(2,1)S(1)}, u32[]{:S(2)}, u32[]{:S(2)}) async-start(bf16[16,32,1024]{2,1,0:T(8,128)(2,1)} %bitcast.9), calls=%async_computation.2 | async-start | bytes 2097152 | tf_op jit(solution)/shard_map/all_to_all | solution.py:38
  169.7 0.5 broadcast.91
  170.2 0.7 reduce.7
  170.9 0.1 eq.52
  171.0 13.0 %all-to-all-done.1 = bf16[16,32,1024]{2,1,0:T(8,128)(2,1)S(1)} async-done(((bf16[16,32,1024]{2,1,0:T(8,128)(2,1)}), bf16[16,32,1024]{2,1,0:T(8,128)(2,1)S(1)}, u32[]{:S(2)}, u32[]{:S(2)}) %all-to-all-start.1) | async-done | bytes 1048608 | tf_op jit(solution)/shard_map/all_to_all | solution.py:38
  183.9 3.2 %multiply_reduce_fusion = bf16[512,16]{0,1:T(8,128)(2,1)S(1)} fusion(bf16[512,1024,1]{1,0,2:T(8,128)(2,1)S(1)} %bitcast.54, bf16[64,16,1024]{2,1,0:T(8,128)(2,1)} %bitcast.62, f32[512,64]{0,1:T(8,128)S(1)} %get-tuple-element.6), kind=kOutput, calls=%fused_computation.6 | convolution fusion | flops 1074782208 | bytes 3293184 | tf_op jit(solution)/shard_map/dot_general | solution.py:46
  187.1 25.2 %psum.7 = bf16[512,16]{0,1:T(8,128)(2,1)S(1)} all-reduce(bf16[512,16]{0,1:T(8,128)(2,1)S(1)} %multiply_reduce_fusion), channel_id=1, replica_groups=mesh['section'=2,'dp'=16,'tensor'=8] {'tensor'}, use_global_device_ids=true, to_apply=%region_6.7 | all-reduce | flops 8192 | bytes 32768 | tf_op jit(solution)/shard_map/psum | solution.py:52
  212.3 0.1 broadcast_multiply_fusion
  212.4 2.3 convolution_convert_fusion
  214.7 5.6 %all-to-all-start.2 = ((bf16[16,32,1024]{2,1,0:T(8,128)(2,1)}), bf16[16,32,1024]{2,1,0:T(8,128)(2,1)S(1)}, u32[]{:S(2)}, u32[]{:S(2)}) async-start(bf16[16,32,1024]{2,1,0:T(8,128)(2,1)} %bitcast.52), calls=%async_computation.3 | async-start | bytes 2097152 | tf_op jit(solution)/shard_map/all_to_all | solution.py:60
  220.3 11.8 %all-to-all-done.2 = bf16[16,32,1024]{2,1,0:T(8,128)(2,1)S(1)} async-done(((bf16[16,32,1024]{2,1,0:T(8,128)(2,1)}), bf16[16,32,1024]{2,1,0:T(8,128)(2,1)S(1)}, u32[]{:S(2)}, u32[]{:S(2)}) %all-to-all-start.2) | async-done | bytes 1048608 | tf_op jit(solution)/shard_map/all_to_all | solution.py:60
  232.1 2.0 gather_fusion
  234.0 1.6 add_convert_fusion
  235.6 8.6 %collective-permute-start = (bf16[256,1024]{1,0:T(8,128)(2,1)S(1)}, bf16[256,1024]{1,0:T(8,128)(2,1)S(1)}, u32[]{:S(2)}, u32[]{:S(2)}) collective-permute-start(bf16[256,1024]{1,0:T(8,128)(2,1)S(1)} %add_convert_fusion), channel_id=1, source_target_pairs={{0,128},{128,0},{1,129},{129,1},{2,130},{130,2},{3,131},{131,3},{4... | collective-permute-start | bytes 1572872 | tf_op jit(solution)/shard_map/ppermute | solution.py:9
  244.2 1.5 collective-permute-done
  245.8 0.8 copy.23
  (11 shorter events, 0.1 us)
Async XLA Ops:
  6.5 205.9 %copy-start = (bf16[1,64,16,1024]{3,2,1,0:T(8,128)(2,1)S(1)}, bf16[1,64,16,1024]{3,2,1,0:T(8,128)(2,1)}, u32[]{:S(2)}) copy-start(bf16[1,64,16,1024]{3,2,1,0:T(8,128)(2,1)} %param.9) | copy-start | bytes 6291460
  6.5 132.2 %all-gather.3.cloned.1.call-start = ((), (), s32[]{:S(2)}) async-start(), calls=%async_computation.5 | async-start | bytes 17825792 | tf_op jit(solution)/shard_map/all_gather | solution.py:66
  7.3 226.8 %reduce-scatter.2.cloned.1.call-start = ((), (), s32[]{:S(2)}) async-start(), calls=%async_computation.4 | async-start | bytes 4718592 | tf_op jit(solution)/shard_map/reduce_scatter | solution.py:69
  151.2 0.7 copy-start.2
  151.2 8.5 %copy-start.1 = (bf16[1,256,1024]{2,1,0:T(8,128)(2,1)S(1)}, bf16[1,256,1024]{2,1,0:T(8,128)(2,1)}, u32[]{:S(2)}) copy-start(bf16[1,256,1024]{2,1,0:T(8,128)(2,1)} %param.6) | copy-start | bytes 1572868
  155.0 11.0 %all-to-all-start = ((s32[16,1,32]{2,1,0:T(1,128)}), s32[16,1,32]{2,1,0:T(1,128)S(1)}, u32[]{:S(2)}, u32[]{:S(2)}) async-start(s32[16,1,32]{2,1,0:T(1,128)} %all_to_all.12), calls=%async_computation.1 | async-start | bytes 16384 | tf_op jit(solution)/shard_map/all_to_all | solution.py:39
  166.0 17.9 %all-to-all-start.1 = ((bf16[16,32,1024]{2,1,0:T(8,128)(2,1)}), bf16[16,32,1024]{2,1,0:T(8,128)(2,1)S(1)}, u32[]{:S(2)}, u32[]{:S(2)}) async-start(bf16[16,32,1024]{2,1,0:T(8,128)(2,1)} %bitcast.9), calls=%async_computation.2 | async-start | bytes 2097152 | tf_op jit(solution)/shard_map/all_to_all | solution.py:38
  214.7 17.4 %all-to-all-start.2 = ((bf16[16,32,1024]{2,1,0:T(8,128)(2,1)}), bf16[16,32,1024]{2,1,0:T(8,128)(2,1)S(1)}, u32[]{:S(2)}, u32[]{:S(2)}) async-start(bf16[16,32,1024]{2,1,0:T(8,128)(2,1)} %bitcast.52), calls=%async_computation.3 | async-start | bytes 2097152 | tf_op jit(solution)/shard_map/all_to_all | solution.py:60
  235.6 10.1 %collective-permute-start = (bf16[256,1024]{1,0:T(8,128)(2,1)S(1)}, bf16[256,1024]{1,0:T(8,128)(2,1)S(1)}, u32[]{:S(2)}, u32[]{:S(2)}) collective-permute-start(bf16[256,1024]{1,0:T(8,128)(2,1)S(1)} %add_convert_fusion), channel_id=1, source_target_pairs={{0,128},{128,0},{1,129},{129,1},{2,130},{130,2},{3,131},{131,3},{4... | collective-permute-start | bytes 1572872 | tf_op jit(solution)/shard_map/ppermute | solution.py:9
Sparse Core Ops, SparseCore 0:
  9.8 128.9 all-gather.2
  151.3 56.0 reduce-scatter.1
where the time goes:
time: 254 us; the launch traced here: 253 us
  waiting for transfers between devices  162 us (64%)
  blocking collectives  25.2 us (10%)
  starting transfers between devices  22.6 us (9%)
  matrix products  17.8 us (7%)
  between operations  13.5 us (5%)
  local copies, waits for them, and re-layouts  9.1 us (4%)
  other arithmetic  3.12 us (1%)
    all_gather x1, waiting for transfers between devices, local(): lax.all_gather(local_weight, 'dp', axis=1, tiled=True)  131 us
    psum x1, blocking collectives, local(): lax.psum(partial_value.astype(jnp.bfloat16), 'tensor').astype(jnp.float32)  25.2 us
    all_to_all x1, waiting for transfers between devices, local(): lax.all_to_all(send_rows, 'dp', split_axis=0, concat_axis=0, tiled=True)  13 us
    dot_general x1, matrix products, local(): jnp.dot(local_rows, lax.all_gather(local_weight, 'dp', axis=1, tiled=True...  12.4 us
    all_to_all x1, waiting for transfers between devices, local(): lax.all_to_all(low_rank.reshape(rows_in.shape), 'dp', split_axis=0, conca...  11.8 us
    ppermute x1, starting transfers between devices, shifted(): lax.ppermute(array, axis, [(i, (i + by) % count) for i in range(count)])  8.6 us
    all_to_all x1, starting transfers between devices, local(): lax.all_to_all(low_rank.reshape(rows_in.shape), 'dp', split_axis=0, conca...  5.58 us
  transfers between devices with their start and end apart: 6, of which 5 were waited for; matrix products, arithmetic and copies ran while one was open for 5% of the time, Pallas kernels for 0%

commit v1 on v0

v1 whole, which is shorter than its diff:
```python
import functools

import jax
import jax.numpy as jnp
from jax import lax
from jax.experimental import pallas as pl
from jax.experimental.pallas import tpu as pltpu
from jax.sharding import PartitionSpec as P

MESH = pl.DeviceIdType.MESH
NX, NY, NZ = 4, 4, 8
ROWS, WIDTH, COLS = 256, 1024, 512
OWNERS, CAP, SLOTS, RANK = 16, 32, 64, 16
NQ = 4
CW = COLS // NQ
STARTS = (0, 0, 4, 6)
ROUNDS = 8 + max(STARTS)
FWD_W = {2: 1, 3: 4}
E1_AT, E2_AT = 7, 9
BF, F32 = jnp.bfloat16, jnp.float32


def remote(src, dst, send, recv, device):
    return pltpu.make_async_remote_copy(
        src_ref=src, dst_ref=dst, send_sem=send, recv_sem=recv, device_id=device, device_id_type=MESH
    )


def dot(a, b, ca, cb):
    return lax.dot_general(a, b, (((ca,), (cb,)), ((), ())), preferred_element_type=F32)


def arrivals(owner, upper):
    hits = lax.broadcasted_iota(jnp.int32, (OWNERS, ROWS), 0) == owner
    count = dot(hits.astype(BF), upper, 1, 0)
    return (jnp.sum(jnp.where(hits, count, 0.0), axis=0, keepdims=True) - 1.0).astype(jnp.int32)


def kernel(
    x_hbm, w_hbm, shrink_hbm, expand_hbm, ids_hbm, out_ref,
    xg, wg, idg, rs, bt, xp, idp, aout, sout, ain, sin, shrink, expand, pin, spread, low, lin,
    loc_sem, x_send, x_recv, id_send, id_recv, w_send, w_recv, p_send, p_recv, f_send, f_recv,
    g_send, g_recv, z_send, z_recv, r_send, r_recv, b_send, b_recv, rs_send, rs_recv,
):
    s = lax.axis_index("section")
    dp = lax.axis_index("dp")
    z = lax.axis_index("tensor")
    x, y = dp // NY, dp % NY
    other = 1 - s
    half = y // 2
    here = lambda xx, yy, zz: (s, xx * NY + yy, zz)
    there = lambda xx, yy, zz: (other, xx * NY + yy, zz)
    z_flip = z + 1 - 2 * (z % 2)

    def local(src, dst, i):
        return pltpu.make_async_copy(src, dst, loc_sem.at[i])

    load_x = local(x_hbm, xg.at[y], 0)
    load_id = local(ids_hbm, idg.at[y], 1)
    load_w = [local(w_hbm.at[:, pl.ds(q * CW, CW)], wg.at[x, q], 4 + q) for q in range(NQ)]
    load_shrink = local(shrink_hbm, shrink, 2)
    load_expand = local(expand_hbm, expand, 3)
    load_x.start()
    load_id.start()
    for q in range(NQ):
        load_w[q].start()
    load_shrink.start()
    load_expand.start()

    barrier = pltpu.get_barrier_semaphore()
    peers = [here(x, (y + d) % NY, z) for d in range(1, NY)]
    peers += [here((x + d) % NX, y, z) for d in range(1, NX)]
    peers += [here(x, y, (z + d) % NZ) for d in range(1, NZ)]
    peers += [there(xx, yy, z) for xx in range(NX) for yy in range(NY)]
    peers += [there(x, yy, z_flip) for yy in range(NY)]
    for peer in peers:
        pl.semaphore_signal(barrier, inc=1, device_id=peer, device_id_type=MESH)
    pl.semaphore_wait(barrier, len(peers))

    started = []

    def start(copy):
        copy.start()
        started.append(copy)

    y_up, y_down, y_far = (y + 1) % NY, (y + NY - 1) % NY, (y + 2) % NY
    x_up, x_down, x_far = (x + 1) % NX, (x + NX - 1) % NX, (x + 2) % NX

    def gather(buf, slots, send, recv, up, down):
        mine, below, above, far = slots
        full_up = remote(buf(mine, None), buf(mine, None), send(0), recv(0), up)
        full_down = remote(buf(mine, None), buf(mine, None), send(1), recv(1), down)
        got_below = remote(buf(below, None), buf(below, None), send(0), recv(0), up)
        got_above = remote(buf(above, None), buf(above, None), send(1), recv(1), down)
        pass_up = remote(buf(below, 0), buf(below, 0), send(2), recv(2), up)
        pass_down = remote(buf(above, 1), buf(above, 1), send(3), recv(3), down)
        got_far0 = remote(buf(far, 0), buf(far, 0), send(2), recv(2), up)
        got_far1 = remote(buf(far, 1), buf(far, 1), send(3), recv(3), down)

        def first():
            start(full_up)
            start(full_down)

        def forward():
            got_below.wait_recv()
            pass_up.start()
            got_above.wait_recv()
            pass_down.start()

        def finish():
            got_far0.wait_recv()
            got_far1.wait_recv()

        def drain():
            pass_up.wait_send()
            pass_down.wait_send()

        return first, forward, finish, drain

    def x_buf(slot, part):
        if part is None:
            return xg.at[slot]
        return xg.at[slot, pl.ds(part * (ROWS // 2), ROWS // 2), :]

    def w_buf(q):
        def buf(slot, part):
            if part is None:
                return wg.at[slot, q]
            return wg.at[slot, q, pl.ds(part * (WIDTH // 2), WIDTH // 2), :]

        return buf

    gx = gather(
        x_buf, (y, y_down, y_up, y_far), lambda i: x_send.at[i], lambda i: x_recv.at[i],
        here(x, y_up, z), here(x, y_down, z),
    )
    gw = [
        gather(
            w_buf(q), (x, x_down, x_up, x_far), lambda i, q=q: w_send.at[q, i], lambda i, q=q: w_recv.at[q, i],
            here(x_up, y, z), here(x_down, y, z),
        )
        for q in range(NQ)
    ]

    load_x.wait()
    gx[0]()
    load_id.wait()
    for d in range(1, NY):
        start(remote(idg.at[y], idg.at[y], id_send.at[d - 1], id_recv.at[d - 1], here(x, (y + d) % NY, z)))
    for q in range(NQ):
        load_w[q].wait()
        gw[q][0]()
    partner = there(x, y, z)
    start(remote(xg.at[y], xp, p_send.at[0], p_recv.at[0], partner))
    start(remote(idg.at[y], idp, p_send.at[1], p_recv.at[1], partner))

    gx[1]()
    gw[0][1]()
    for d in range(1, NY):
        src_y = (y + NY - d) % NY
        remote(idg.at[src_y], idg.at[src_y], id_send.at[d - 1], id_recv.at[d - 1], partner).wait_recv()
    gx[2]()

    upper = (
        lax.broadcasted_iota(jnp.int32, (ROWS, ROWS), 0) <= lax.broadcasted_iota(jnp.int32, (ROWS, ROWS), 1)
    ).astype(BF)
    codes, slot_rows = [], []
    for yb in range(NY):
        owner = idg[yb, 0:1, :]
        code = (owner >> 2) * (NY * CAP) + yb * CAP + arrivals(owner, upper)
        codes.append(jnp.where((owner & 3) == y, code, -1))
        slot_rows.append(idg[yb, 1:2, :])
    rows_of_x = NY * CAP
    for yb in range(NY):
        pick = (lax.broadcasted_iota(jnp.int32, (NX * rows_of_x, ROWS), 0) == codes[yb]).astype(BF)
        sub = jnp.concatenate(
            [pick[xx * rows_of_x + yb * CAP : xx * rows_of_x + (yb + 1) * CAP] for xx in range(NX)], axis=0
        )
        rows = dot(sub, xg[yb], 1, 0).astype(BF)
        for xx in range(NX):
            aout[xx, yb * CAP : (yb + 1) * CAP, :] = rows[xx * CAP : (xx + 1) * CAP]
        slot_block = jnp.broadcast_to(slot_rows[yb].astype(F32).astype(BF), (8, ROWS))
        chosen = dot(slot_block, pick, 1, 1)
        for xx in range(NX):
            part = chosen[:, xx * rows_of_x : (xx + 1) * rows_of_x]
            if yb == 0:
                sout[xx] = part
            else:
                sout[xx] = sout[xx] + part
    for d in range(1, NX):
        to = (x + d) % NX
        start(remote(aout.at[to], ain.at[x], f_send.at[d - 1], f_recv.at[d - 1], here(to, y, z)))
        start(remote(sout.at[to], sin.at[x], g_send.at[d - 1], g_recv.at[d - 1], here(to, y, z)))
    ain[x] = aout[x]
    sin[x] = sout[x]

    gw[0][2]()
    gw[1][1]()
    gw[1][2]()

    def rs_parts(q, direction, t):
        if direction == 0:
            block = lax.rem(z - 1 - t + 2 * NZ, NZ)
            to = here(x, y, (z + 1) % NZ)
        else:
            block = lax.rem(z + 1 + t, NZ)
            to = here(x, y, (z + NZ - 1) % NZ)
        aligned = 1 - (block + half) % 2
        off = aligned * direction + (1 - aligned) * (3 - direction)
        return block, lax.rem(y + off, NY), to

    def rs_copy(q, direction, t, to):
        return remote(
            rs.at[direction, q, t], rs.at[direction, q, t + 1],
            rs_send.at[direction, q, t], rs_recv.at[direction, q, t], to,
        )

    def last_copy(q, direction):
        _, row_block, _ = rs_parts(q, direction, NZ - 1)
        dest = there(x, row_block, 2 * (z // 2) + half)
        return remote(
            rs.at[direction, q, NZ - 1], bt.at[y % 2, q], b_send.at[direction, q], b_recv.at[y % 2, q], dest
        )

    def rs_step(q, direction, t):
        block, row_block, to = rs_parts(q, direction, t)
        part = dot(xg[row_block], wg[block // 2, q], 1, 0)

        @pl.when(t == 0)
        def _():
            rs[direction, q, 0] = part.astype(BF)

        @pl.when(t > 0)
        def _():
            rs_copy_in = remote(
                rs.at[direction, q, t], rs.at[direction, q, t],
                rs_send.at[direction, q, t - 1], rs_recv.at[direction, q, t - 1], to,
            )
            rs_copy_in.wait_recv()
            rs[direction, q, t] = (part + rs[direction, q, t].astype(F32)).astype(BF)

        @pl.when(t < NZ - 1)
        def _():
            rs_copy(q, direction, t, to).start()

        @pl.when(t == NZ - 1)
        def _():
            last_copy(q, direction).start()

    def slots_of():
        return jnp.concatenate([sin[xx, 0:1, :] for xx in range(NX)], axis=1).astype(jnp.int32)

    def shrink_part():
        load_shrink.wait()
        for d in range(1, NX):
            src = (x + NX - d) % NX
            remote(ain.at[src], ain.at[src], f_send.at[d - 1], f_recv.at[d - 1], partner).wait_recv()
            remote(sin.at[src], sin.at[src], g_send.at[d - 1], g_recv.at[d - 1], partner).wait_recv()
        slots = slots_of()
        rows = ain[...].reshape(NX * rows_of_x, WIDTH)
        total = jnp.zeros((RANK, NX * rows_of_x), F32)
        group = 16
        for c in range(SLOTS // group):
            projected = dot(shrink[c * group * RANK : (c + 1) * group * RANK, :], rows, 1, 1)
            for k in range(group):
                total = total + jnp.where(
                    slots == c * group + k, projected[k * RANK : (k + 1) * RANK], 0.0
                )
        pin[z] = total.astype(BF)
        for d in range(1, NZ):
            remote(pin.at[z], pin.at[z], z_send.at[d - 1], z_recv.at[d - 1], here(x, y, (z + d) % NZ)).start()

    def return_copy(xx, yb):
        return remote(
            low.at[xx, pl.ds(yb * CAP, CAP), :], lin.at[dp], r_send.at[xx * NY + yb], r_recv.at[dp], there(xx, yb, z)
        )

    def expand_part():
        load_expand.wait()
        for d in range(1, NZ):
            src = (z + NZ - d) % NZ
            remote(pin.at[src], pin.at[src], z_send.at[d - 1], z_recv.at[d - 1], partner).wait_recv()
        slots = slots_of()
        total = pin[0].astype(F32)
        for k in range(1, NZ):
            total = total + pin[k].astype(F32)
        for k in range(SLOTS):
            spread[k * RANK : (k + 1) * RANK, :] = jnp.where(slots == k, total, 0.0).astype(BF)
        for d in range(NX):
            for xx in range(d, d + 1):
                part = dot(spread[:, xx * rows_of_x : (xx + 1) * rows_of_x], expand[...], 0, 0)
                low[xx] = part.astype(BF)
                for yb in range(NY):
                    return_copy(xx, yb).start()

    def round_of(i, carry):
        for q in range(NQ):
            t = i - STARTS[q]
            if STARTS[q] > 0:
                @pl.when(t == 0)
                def _():
                    gw[q][2]()

            @pl.when((t >= 0) & (t < NZ))
            def _():
                for direction in range(2):
                    rs_step(q, direction, t)

        for q, at in FWD_W.items():
            @pl.when(i == at)
            def _():
                gw[q][1]()

        pl.when(i == E1_AT)(shrink_part)
        pl.when(i == E2_AT)(expand_part)
        return carry

    lax.fori_loop(0, ROUNDS, round_of, 0)

    remote(xg.at[y], xp, p_send.at[0], p_recv.at[0], partner).wait_recv()
    remote(idg.at[y], idp, p_send.at[1], p_recv.at[1], partner).wait_recv()
    owner = idp[0:1, :]
    code = owner * CAP + arrivals(owner, upper)
    pick = (lax.broadcasted_iota(jnp.int32, (OWNERS * CAP, ROWS), 0) == code).astype(BF)
    for o in range(OWNERS):
        remote(lin.at[o], lin.at[o], r_send.at[o], r_recv.at[o], partner).wait_recv()
    got = lin[...].reshape(OWNERS * CAP, WIDTH)
    for p in range(2):
        for q in range(NQ):
            remote(bt.at[p, q], bt.at[p, q], b_send.at[0, q], b_recv.at[p, q], partner).wait_recv()
    for c in range(WIDTH // 256):
        cols = slice(c * 256, (c + 1) * 256)
        rows = dot(pick, got[:, cols], 0, 0)
        p, q = (c * 256) // COLS, ((c * 256) % COLS) // CW
        base = jnp.concatenate([bt[p, q + k] for k in range(256 // CW)], axis=1)
        out_ref[:, cols] = (xp[:, cols].astype(F32) + base.astype(F32) + rows).astype(BF)

    for copy in started:
        copy.wait_send()
    gx[3]()
    for q in range(NQ):
        gw[q][3]()
        for direction in range(2):
            for t in range(NZ - 1):
                rs_copy(q, direction, t, partner).wait_send()
            last_copy(q, direction).wait_send()
    for d in range(1, NZ):
        remote(pin.at[z], pin.at[z], z_send.at[d - 1], z_recv.at[d - 1], partner).wait_send()
    for xx in range(NX):
        for yb in range(NY):
            return_copy(xx, yb).wait_send()


def local_part(hidden_states, base_weight, shrink_weight, expand_weight, owner_ids, adapter_slots):
    ids = jnp.concatenate(
        [owner_ids.reshape(1, ROWS), adapter_slots.reshape(1, ROWS), jnp.zeros((6, ROWS), jnp.int32)], axis=0
    )
    dma = pltpu.SemaphoreType.DMA
    any_spec = pl.BlockSpec(memory_space=pl.ANY)
    rows_of_x = NY * CAP
    out = pl.pallas_call(
        kernel,
        out_shape=jax.ShapeDtypeStruct((ROWS, WIDTH), BF),
        in_specs=[any_spec] * 5,
        out_specs=pl.BlockSpec(memory_space=pltpu.VMEM),
        scratch_shapes=[
            pltpu.VMEM((NY, ROWS, WIDTH), BF),
            pltpu.VMEM((NX, NQ, WIDTH, CW), BF),
            pltpu.VMEM((NY, 8, ROWS), jnp.int32),
            pltpu.VMEM((2, NQ, NZ, ROWS, CW), BF),
            pltpu.VMEM((2, NQ, ROWS, CW), BF),
            pltpu.VMEM((ROWS, WIDTH), BF),
            pltpu.VMEM((8, ROWS), jnp.int32),
            pltpu.VMEM((NX, rows_of_x, WIDTH), BF),
            pltpu.VMEM((NX, 8, rows_of_x), F32),
            pltpu.VMEM((NX, rows_of_x, WIDTH), BF),
            pltpu.VMEM((NX, 8, rows_of_x), F32),
            pltpu.VMEM((SLOTS * RANK, WIDTH), BF),
            pltpu.VMEM((SLOTS * RANK, WIDTH), BF),
            pltpu.VMEM((NZ, RANK, NX * rows_of_x), BF),
            pltpu.VMEM((SLOTS * RANK, NX * rows_of_x), BF),
            pltpu.VMEM((NX, rows_of_x, WIDTH), BF),
            pltpu.VMEM((OWNERS, CAP, WIDTH), BF),
            dma((4 + NQ,)),
            dma((4,)), dma((4,)),
            dma((NY - 1,)), dma((NY - 1,)),
            dma((NQ, 4)), dma((NQ, 4)),
            dma((2,)), dma((2,)),
            dma((NX - 1,)), dma((NX - 1,)),
            dma((NX - 1,)), dma((NX - 1,)),
            dma((NZ - 1,)), dma((NZ - 1,)),
            dma((OWNERS,)), dma((OWNERS,)),
            dma((2, NQ)), dma((2, NQ)),
            dma((2, NQ, NZ)), dma((2, NQ, NZ)),
        ],
        compiler_params=pltpu.CompilerParams(
            collective_id=0, has_side_effects=True, vmem_limit_bytes=56 << 20
        ),
    )(
        hidden_states[0],
        base_weight[0],
        shrink_weight[0].reshape(SLOTS * RANK, WIDTH),
        expand_weight[0].reshape(SLOTS * RANK, WIDTH),
        ids,
    )
    return out[None]


def solution(mesh):
    return jax.shard_map(
        local_part,
        mesh=mesh,
        in_specs=(
            P("section", "dp", "tensor"),
            P("section", "tensor", "dp"),
            P("section", "dp", None, "tensor"),
            P("section", "dp", None, "tensor"),
            P("section", "dp", None),
            P("section", "dp"),
        ),
        out_specs=P("section", "dp", "tensor"),
        check_vma=False,
    )
```

time: 254 us -> 126 us (0.50)
  waiting for transfers between devices: 162 us -> 0 us
  Pallas kernels: 0 us -> 122 us
  blocking collectives: 25.2 us -> 0 us
  starting transfers between devices: 22.6 us -> 0 us
  matrix products: 17.8 us -> 0 us
  between operations: 13.5 us -> 0.01 us
  local copies, waits for them, and re-layouts: 9.1 us -> 1.95 us
    all_gather x1 -> x0, waiting for transfers between devices: 131 us -> none  [local(): lax.all_gather(local_weight, 'dp', axis=1, tiled=True)]
    pallas_call x0 -> x1, Pallas kernels: none -> 122 us  [local_part(): pl.pallas_call(kernel, out_shape=jax.ShapeDtypeStruct((ROWS, WIDTH), BF),...]
    all_to_all x3 -> x0, waiting for transfers between devices: 28.4 us -> none  [the longest x1 13 us: local(): lax.all_to_all(send_rows, 'dp', split_axis=0, concat_axis=0, tiled=True)]
    psum x1 -> x0, blocking collectives: 25.2 us -> none  [local(): lax.psum(partial_value.astype(jnp.bfloat16), 'tensor').astype(jnp.float32)]
    dot_general x3 -> x0, matrix products: 17.8 us -> none  [the longest x1 12.4 us: local(): jnp.dot(local_rows, lax.all_gather(local_weight, 'dp', axis=1, tiled=True...]
    all_to_all x3 -> x0, starting transfers between devices: 13.9 us -> none  [the longest x1 5.58 us: local(): lax.all_to_all(low_rank.reshape(rows_in.shape), 'dp', split_axis=0, conca...]
    ppermute x1 -> x0, starting transfers between devices: 8.6 us -> none  [shifted(): lax.ppermute(array, axis, [(i, (i + by) % count) for i in range(count)])]
    scatter x2 -> x0, local copies, waits for them, and re-layouts: 4.22 us -> none  [the longest x1 2.66 us: local(): send_rows = jnp.zeros((owner_count * capacity, feature_width), jnp.bfloat...]
  transfers between devices with their start and end apart: 6 -> 0, of which waited for: 5 -> 0; matrix products, arithmetic and copies ran while one was open for 5% -> 0% of each run, Pallas kernels for 0% -> 0%
where the time goes in v1:
time: 126 us; the launch traced here: 125 us
  Pallas kernels  122 us (97%)
  local copies, waits for them, and re-layouts  1.95 us (2%)
  other arithmetic  1.36 us (1%)
    pallas_call x1, Pallas kernels, local_part(): pl.pallas_call(kernel, out_shape=jax.ShapeDtypeStruct((ROWS, WIDTH), BF),...  122 us

profile of v1, /device:TPU:1, one launch (start us, length us, event | category | flops | bytes accessed | tf_op | source)
XLA Modules:
  0.0 124.9 jit_solution(6264653847890054006)
XLA Ops:
  0.0 0.1 pad.2.clone
  0.1 1.4 %add_add_fusion.ids_hbm = s32[8,256]{1,0:T(8,128)} fusion(s32[1,256]{1,0:T(1,128)} %param.11, s32[1,256]{1,0:T(1,128)} %bitcast.11, s32[8]{0:T(128)S(1)} %pad.2.clone), kind=kLoop, calls=%fused_computation | loop fusion | flops 4096 | bytes 10272 | tf_op jit(solution)/shard_map/concatenate | solution.py:355
  1.4 121.6 %shard_map.64 = bf16[256,1024]{1,0:T(8,128)(2,1)} custom-call(bf16[256,1024]{1,0:T(8,128)(2,1)} %bitcast.10, bf16[1024,512]{1,0:T(8,128)(2,1)} %bitcast.9, bf16[1024,1024]{1,0:T(8,128)(2,1)} %bitcast.7, bf16[1024,1024]{1,0:T(8,128)(2,1)} %bitcast.8, s32[8,256]{1,0:T(8,128)} %add_add_fusion.ids_hbm), custom_call_target="tpu_custom_call" | custom-call | tf_op jit(solution)/shard_map/pallas_call | solution.py:361
  123.1 1.9 %copy.8 = bf16[1,256,1024]{2,1,0:T(8,128)(2,1)} copy(bf16[1,256,1024]{2,1,0:T(8,128)(2,1)} %bitcast.6) | data formatting | bytes 1048576
  (1 shorter events, 0.0 us)

commit v2 on v0

v2 whole, which is shorter than its diff:
```python
import functools

import jax
import jax.numpy as jnp
from jax import lax
from jax.experimental import pallas as pl
from jax.experimental.pallas import tpu as pltpu
from jax.sharding import PartitionSpec as P

MESH = pl.DeviceIdType.MESH
NX, NY, NZ = 4, 4, 8
ROWS, WIDTH, COLS = 256, 1024, 512
OWNERS, CAP, SLOTS, RANK = 16, 32, 64, 16
NQ = 4
CW = COLS // NQ
GROUP = NY * CAP
FLOWS = NQ * NY
STEPS = 3
LAGS = (0, 2, 5, 8, 10)
ROUNDS = FLOWS + LAGS[4]
SEND_W = {2: 2, 3: 6}
PASS_W = {1: 1, 2: 5, 3: 9}
ROUTE_AT = 9
SHRINK_AT = (15, 15, 16, 16)
EXPAND_AT = (19, 19, 20, 20)
PARTS = 4
BF, F32 = jnp.bfloat16, jnp.float32


def remote(src, dst, send, recv, device):
    return pltpu.make_async_remote_copy(
        src_ref=src, dst_ref=dst, send_sem=send, recv_sem=recv, device_id=device, device_id_type=MESH
    )


def dot(a, b, ca, cb):
    return lax.dot_general(a, b, (((ca,), (cb,)), ((), ())), preferred_element_type=F32)


def arrivals(owner, upper):
    hits = lax.broadcasted_iota(jnp.int32, (OWNERS, ROWS), 0) == owner
    count = dot(hits.astype(BF), upper, 1, 0)
    return (jnp.sum(jnp.where(hits, count, 0.0), axis=0, keepdims=True) - 1.0).astype(jnp.int32)


def kernel(
    x_hbm, w_hbm, shrink_hbm, expand_hbm, ids_hbm, out_ref,
    xg, wg, idg, rs, bt, xp, idp, aout, sout, ain, sin, shrink, expand, total, pin, spread, low, lin,
    loc_sem, x_send, x_recv, id_send, id_recv, w_send, w_recv, p_send, p_recv, f_send, f_recv,
    g_send, g_recv, z_send, z_recv, r_send, r_recv, b_send, b_recv, rs_send, rs_recv,
):
    s = lax.axis_index("section")
    dp = lax.axis_index("dp")
    z = lax.axis_index("tensor")
    x, y = dp // NY, dp % NY
    u, v = y, x
    place = lambda uu, vv: vv * NY + uu
    here = lambda uu, vv, zz: (s, place(uu, vv), zz)
    there = lambda uu, vv, zz: (1 - s, place(uu, vv), zz)
    odd = (z + u // 2) % 2
    partner = (1 - s, dp, z)

    def local(src, dst, i):
        return pltpu.make_async_copy(src, dst, loc_sem.at[i])

    block_of = lambda b: xg.at[pl.ds(pl.multiple_of(b * ROWS, ROWS), ROWS), :]
    load_x = local(x_hbm, block_of(u), 0)
    load_id = local(ids_hbm, idg.at[u], 1)
    load_w = [local(w_hbm.at[:, pl.ds(q * CW, CW)], wg.at[v, q], 4 + q) for q in range(NQ)]
    load_shrink = local(shrink_hbm, shrink, 2)
    load_expand = local(expand_hbm, expand, 3)
    load_x.start()
    for q in range(NQ):
        load_w[q].start()
    load_id.start()
    load_shrink.start()
    load_expand.start()

    barrier = pltpu.get_barrier_semaphore()
    peers = [here((u + d) % NY, v, z) for d in range(1, NY)]
    peers += [here(u, (v + d) % NX, z) for d in range(1, NX)]
    peers += [here(u, v, (z + d) % NZ) for d in range(1, NZ)]
    peers += [(1 - s, o, z) for o in range(OWNERS)]
    for peer in peers:
        pl.semaphore_signal(barrier, inc=1, device_id=peer, device_id_type=MESH)
    pl.semaphore_wait(barrier, len(peers))

    started = []

    def start(copy):
        copy.start()
        started.append(copy)

    def gather(buf, slots, send, recv, up, down):
        mine, below, above, far = slots
        sends = [remote(buf(mine, h), buf(mine, h), send(i), recv(i), to) for i, (h, to) in enumerate(
            [(0, up), (1, down), (1, up), (0, down)])]
        arrive = [remote(buf(slot, h), buf(slot, h), send(i), recv(i), up) for i, (slot, h) in enumerate(
            [(below, 0), (above, 1), (below, 1), (above, 0)])]
        pass_up = remote(buf(below, 0), buf(below, 0), send(4), recv(4), up)
        pass_down = remote(buf(above, 1), buf(above, 1), send(5), recv(5), down)
        far_up = remote(buf(far, 0), buf(far, 0), send(4), recv(4), up)
        far_down = remote(buf(far, 1), buf(far, 1), send(5), recv(5), down)

        def first():
            for copy in sends:
                copy.start()

        def forward():
            arrive[0].wait_recv()
            pass_up.start()
            arrive[1].wait_recv()
            pass_down.start()

        def finish_below():
            arrive[2].wait_recv()

        def finish_above():
            arrive[3].wait_recv()

        def finish_far():
            far_up.wait_recv()
            far_down.wait_recv()

        def finish():
            finish_below()
            finish_above()
            finish_far()

        def drain():
            for copy in sends:
                copy.wait_send()
            pass_up.wait_send()
            pass_down.wait_send()

        return first, forward, finish_below, finish_above, finish_far, finish, drain

    u_up, u_down, u_far = (u + 1) % NY, (u + NY - 1) % NY, (u + 2) % NY
    v_up, v_down, v_far = (v + 1) % NX, (v + NX - 1) % NX, (v + 2) % NX
    x_buf = lambda slot, h: xg.at[pl.ds(pl.multiple_of(slot * ROWS + h * (ROWS // 2), ROWS // 2), ROWS // 2), :]
    w_buf = lambda q: lambda slot, h: wg.at[slot, q, pl.ds(h * (WIDTH // 2), WIDTH // 2), :]
    gx = gather(
        x_buf, (u, u_down, u_up, u_far), lambda i: x_send.at[i], lambda i: x_recv.at[i],
        here(u_up, v, z), here(u_down, v, z),
    )
    gw = lambda q: gather(
        w_buf(q), (v, v_down, v_up, v_far), lambda i: w_send.at[q, i], lambda i: w_recv.at[q, i],
        here(u, v_up, z), here(u, v_down, z),
    )

    load_x.wait()
    gx[0]()
    for q in range(NQ):
        load_w[q].wait()
        if q not in SEND_W:
            gw(q)[0]()
    load_id.wait()
    for d in range(1, NY):
        start(remote(idg.at[u], idg.at[u], id_send.at[d - 1], id_recv.at[d - 1], here((u + d) % NY, v, z)))
    start(remote(block_of(u), xp, p_send.at[0], p_recv.at[0], partner))
    start(remote(idg.at[u], idp, p_send.at[1], p_recv.at[1], partner))

    gx[1]()
    gw(0)[1]()

    upper = (
        lax.broadcasted_iota(jnp.int32, (ROWS, ROWS), 0) <= lax.broadcasted_iota(jnp.int32, (ROWS, ROWS), 1)
    ).astype(BF)

    def route():
        for d in range(1, NY):
            src = (u + NY - d) % NY
            remote(idg.at[src], idg.at[src], id_send.at[d - 1], id_recv.at[d - 1], partner).wait_recv()
        for b in range(NY):
            owner = idg[b, 0:1, :]
            code = jnp.where((owner & 3) == u, (owner >> 2) * CAP + arrivals(owner, upper), -1)
            pick = (lax.broadcasted_iota(jnp.int32, (NX * CAP, ROWS), 0) == code).astype(BF)
            rows = dot(pick, xg[b * ROWS : (b + 1) * ROWS, :], 1, 0).astype(BF)
            for vv in range(NX):
                aout[vv, b * CAP : (b + 1) * CAP, :] = rows[vv * CAP : (vv + 1) * CAP]
            place_in = (
                lax.broadcasted_iota(jnp.int32, (NX * GROUP, ROWS), 0)
                == jnp.where(code < 0, -1, (code >> 5) * GROUP + b * CAP + (code & 31))
            ).astype(BF)
            slot_block = jnp.broadcast_to(idg[b, 1:2, :].astype(F32).astype(BF), (8, ROWS))
            chosen = dot(slot_block, place_in, 1, 1)
            for vv in range(NX):
                part = chosen[:, vv * GROUP : (vv + 1) * GROUP]
                sout[vv] = part if b == 0 else sout[vv] + part
        for d in range(1, NX):
            to = (v + d) % NX
            route_copy(d, to).start()
            slot_copy(d, to).start()
        ain[v] = aout[v]
        sin[v] = sout[v]

    def route_copy(d, to):
        return remote(aout.at[to], ain.at[v], f_send.at[d - 1], f_recv.at[d - 1], here(u, to, z))

    def slot_copy(d, to):
        return remote(sout.at[to], sin.at[v], g_send.at[d - 1], g_recv.at[d - 1], here(u, to, z))

    def row_block(f):
        r = f % NY
        return (u + ((r + 3) // 4) * ((r + 1) % 3 + 1)) % NY

    def ring_copy(f, direction, p):
        to = here(u, v, (z + 1) % NZ if direction == 0 else (z + NZ - 1) % NZ)
        return remote(
            rs.at[direction, f, p], rs.at[direction, f, p + odd],
            rs_send.at[direction, f, p], rs_recv.at[direction, f, p + odd], to,
        )

    def arrived(f, direction, p):
        remote(
            rs.at[direction, f, p], rs.at[direction, f, p],
            rs_send.at[direction, f, p], rs_recv.at[direction, f, p], partner,
        ).wait_recv()
        return rs[direction, f, p].astype(F32)

    def last_copy(f):
        return remote(
            rs.at[0, f, 2], bt.at[u % 2, f // NY], b_send.at[f], b_recv.at[u % 2, f // NY], there(row_block(f), v, z)
        )

    def product(f, root):
        rows = pl.ds(pl.multiple_of(row_block(f) * ROWS, ROWS), ROWS)
        return dot(xg[rows, :], wg[root // 2, f // NY], 1, 0)

    def in_turn(f):
        return (f >= 0) & (f < FLOWS)

    def first_direction(f):
        return f % 2

    def tile_step(i):
        @pl.when((odd == 0) & in_turn(i))
        def _():
            part = product(i, (z + 4) % NZ).astype(BF)
            for direction in range(2):
                @pl.when(first_direction(i) == direction)
                def _():
                    rs[direction, i, 0] = part
                    ring_copy(i, direction, 0).start()

        f3 = i - LAGS[1]

        @pl.when((odd == 1) & in_turn(f3))
        def _():
            for direction in range(2):
                root = (z + 3) % NZ if direction == 0 else (z + NZ - 3) % NZ
                part = product(f3, root)

                @pl.when(first_direction(f3) == direction)
                def _():
                    rs[direction, f3, 0] = (part + arrived(f3, direction, 0)).astype(BF)

                @pl.when(first_direction(f3) != direction)
                def _():
                    rs[direction, f3, 0] = part.astype(BF)

                ring_copy(f3, direction, 0).start()

        away = 2 - odd
        f1 = i - LAGS[2] - odd * (LAGS[3] - LAGS[2])

        @pl.when(in_turn(f1))
        def _():
            for direction in range(2):
                root = (z + away) % NZ if direction == 0 else (z + NZ - away) % NZ
                part = product(f1, root)
                rs[direction, f1, 1] = (part + arrived(f1, direction, 1)).astype(BF)
                ring_copy(f1, direction, 1).start()

        f0 = i - LAGS[4]

        @pl.when((odd == 0) & in_turn(f0))
        def _():
            part = product(f0, z)
            part = part + arrived(f0, 0, 2)
            rs[0, f0, 2] = (part + arrived(f0, 1, 2)).astype(BF)
            last_copy(f0).start()

    def shrink_part(c):
        if c == 0:
            load_shrink.wait()
            for d in range(1, NX):
                src = (v + NX - d) % NX
                remote(ain.at[src], ain.at[src], f_send.at[d - 1], f_recv.at[d - 1], partner).wait_recv()
                remote(sin.at[src], sin.at[src], g_send.at[d - 1], g_recv.at[d - 1], partner).wait_recv()
            total[...] = jnp.zeros_like(total)

        count = SLOTS // PARTS
        projected = dot(
            shrink[pl.ds(c * (count * RANK), count * RANK), :], ain[...].reshape(NX * GROUP, WIDTH), 1, 1
        )
        for vv in range(NX):
            slots = sin[vv, 0:1, :].astype(jnp.int32) - c * count
            sums = total[vv]
            for k in range(count):
                sums = sums + jnp.where(
                    slots == k, projected[k * RANK : (k + 1) * RANK, vv * GROUP : (vv + 1) * GROUP], 0.0
                )
            total[vv] = sums

        if c == PARTS - 1:
            pin[z] = total[...].astype(BF)
            for d in range(1, NZ):
                sum_copy(d).start()

    def sum_copy(d):
        return remote(pin.at[z], pin.at[z], z_send.at[d - 1], z_recv.at[d - 1], here(u, v, (z + d) % NZ))

    def return_copy(vv, b):
        return remote(
            low.at[vv, pl.ds(b * CAP, CAP), :], lin.at[dp], r_send.at[vv, b], r_recv.at[dp], there(b, vv, z)
        )

    def expand_part(vv):
        if vv == 0:
            load_expand.wait()
            for d in range(1, NZ):
                src = (z + NZ - d) % NZ
                remote(pin.at[src], pin.at[src], z_send.at[d - 1], z_recv.at[d - 1], partner).wait_recv()

        sums = pin[0, vv].astype(F32)
        for k in range(1, NZ):
            sums = sums + pin[k, vv].astype(F32)
        slots = sin[vv, 0:1, :].astype(jnp.int32)
        for k in range(SLOTS):
            spread[k * RANK : (k + 1) * RANK, :] = jnp.where(slots == k, sums, 0.0).astype(BF)
        low[vv] = dot(spread[...], expand[...], 0, 0).astype(BF)
        for b in range(NY):
            return_copy(vv, b).start()

    def round_of(j, carry):
        @pl.when(in_turn(j) & (j % NY == 0))
        def _():
            gw(j // NY)[5]()

        for f in range(1, NY):
            pl.when(j == f)(gx[1 + f])

        for chunk, at in PASS_W.items():
            pl.when(j == at)(gw(chunk)[1])
        for chunk, at in SEND_W.items():
            pl.when(j == at)(gw(chunk)[0])

        tile_step(j)

        pl.when(j == ROUTE_AT)(route)
        for c in range(PARTS):
            pl.when(j == SHRINK_AT[c])(functools.partial(shrink_part, c))
        for vv in range(NX):
            pl.when(j == EXPAND_AT[vv])(functools.partial(expand_part, vv))
        return carry

    lax.fori_loop(0, ROUNDS, round_of, 0)

    remote(block_of(u), xp, p_send.at[0], p_recv.at[0], partner).wait_recv()
    remote(idg.at[u], idp, p_send.at[1], p_recv.at[1], partner).wait_recv()
    owner = idp[0:1, :]
    code = owner * CAP + arrivals(owner, upper)
    pick = (lax.broadcasted_iota(jnp.int32, (OWNERS * CAP, ROWS), 0) == code).astype(BF)
    for o in range(OWNERS):
        remote(lin.at[o], lin.at[o], r_send.at[0, 0], r_recv.at[o], partner).wait_recv()
    got = lin[...].reshape(OWNERS * CAP, WIDTH)
    for q in range(NQ):
        for p in range(2):
            remote(bt.at[p, q], bt.at[p, q], b_send.at[q], b_recv.at[p, q], partner).wait_recv()
    for c in range(WIDTH // 256):
        cols = slice(c * 256, (c + 1) * 256)
        rows = dot(pick, got[:, cols], 0, 0)
        p, q = (c * 256) // COLS, ((c * 256) % COLS) // CW
        base = jnp.concatenate([bt[p, q + k] for k in range(256 // CW)], axis=1)
        out_ref[:, cols] = (xp[:, cols].astype(F32) + base.astype(F32) + rows).astype(BF)

    for copy in started:
        copy.wait_send()
    gx[6]()
    for q in range(NQ):
        gw(q)[6]()

    def drain_flow(f, carry):
        for direction in range(2):
            pl.when((odd == 1) | (first_direction(f) == direction))(
                lambda: ring_copy(f, direction, 0).wait_send()
            )
            ring_copy(f, direction, 1).wait_send()
        pl.when(odd == 0)(lambda: last_copy(f).wait_send())
        return carry

    lax.fori_loop(0, FLOWS, drain_flow, 0)
    for d in range(1, NX):
        route_copy(d, (v + d) % NX).wait_send()
        slot_copy(d, (v + d) % NX).wait_send()
    for d in range(1, NZ):
        sum_copy(d).wait_send()
    for vv in range(NX):
        for b in range(NY):
            return_copy(vv, b).wait_send()


def local_part(hidden_states, base_weight, shrink_weight, expand_weight, owner_ids, adapter_slots):
    ids = jnp.concatenate(
        [owner_ids.reshape(1, ROWS), adapter_slots.reshape(1, ROWS), jnp.zeros((6, ROWS), jnp.int32)], axis=0
    )
    dma = pltpu.SemaphoreType.DMA
    any_spec = pl.BlockSpec(memory_space=pl.ANY)
    out = pl.pallas_call(
        kernel,
        out_shape=jax.ShapeDtypeStruct((ROWS, WIDTH), BF),
        in_specs=[any_spec] * 5,
        out_specs=pl.BlockSpec(memory_space=pltpu.VMEM),
        scratch_shapes=[
            pltpu.VMEM((NY * ROWS, WIDTH), BF),
            pltpu.VMEM((NX, NQ, WIDTH, CW), BF),
            pltpu.VMEM((NY, 8, ROWS), jnp.int32),
            pltpu.VMEM((2, FLOWS, STEPS, ROWS, CW), BF),
            pltpu.VMEM((2, NQ, ROWS, CW), BF),
            pltpu.VMEM((ROWS, WIDTH), BF),
            pltpu.VMEM((8, ROWS), jnp.int32),
            pltpu.VMEM((NX, GROUP, WIDTH), BF),
            pltpu.VMEM((NX, 8, GROUP), F32),
            pltpu.VMEM((NX, GROUP, WIDTH), BF),
            pltpu.VMEM((NX, 8, GROUP), F32),
            pltpu.VMEM((SLOTS * RANK, WIDTH), BF),
            pltpu.VMEM((SLOTS * RANK, WIDTH), BF),
            pltpu.VMEM((NX, RANK, GROUP), F32),
            pltpu.VMEM((NZ, NX, RANK, GROUP), BF),
            pltpu.VMEM((SLOTS * RANK, GROUP), BF),
            pltpu.VMEM((NX, GROUP, WIDTH), BF),
            pltpu.VMEM((OWNERS, CAP, WIDTH), BF),
            dma((4 + NQ,)),
            dma((6,)), dma((6,)),
            dma((NY - 1,)), dma((NY - 1,)),
            dma((NQ, 6)), dma((NQ, 6)),
            dma((2,)), dma((2,)),
            dma((NX - 1,)), dma((NX - 1,)),
            dma((NX - 1,)), dma((NX - 1,)),
            dma((NZ - 1,)), dma((NZ - 1,)),
            dma((NX, NY)), dma((OWNERS,)),
            dma((FLOWS,)), dma((2, NQ)),
            dma((2, FLOWS, STEPS)), dma((2, FLOWS, STEPS)),
        ],
        compiler_params=pltpu.CompilerParams(
            collective_id=0, has_side_effects=True, vmem_limit_bytes=56 << 20
        ),
    )(
        hidden_states[0],
        base_weight[0],
        shrink_weight[0].reshape(SLOTS * RANK, WIDTH),
        expand_weight[0].reshape(SLOTS * RANK, WIDTH),
        ids,
    )
    return out[None]


def solution(mesh):
    return jax.shard_map(
        local_part,
        mesh=mesh,
        in_specs=(
            P("section", "dp", "tensor"),
            P("section", "tensor", "dp"),
            P("section", "dp", None, "tensor"),
            P("section", "dp", None, "tensor"),
            P("section", "dp", None),
            P("section", "dp"),
        ),
        out_specs=P("section", "dp", "tensor"),
        check_vma=False,
    )
```

time: 254 us -> 101 us (0.40)
  waiting for transfers between devices: 162 us -> 0 us
  Pallas kernels: 0 us -> 96.8 us
  blocking collectives: 25.2 us -> 0 us
  starting transfers between devices: 22.6 us -> 0 us
  matrix products: 17.8 us -> 0 us
  between operations: 13.5 us -> 0.01 us
  local copies, waits for them, and re-layouts: 9.1 us -> 1.95 us
    all_gather x1 -> x0, waiting for transfers between devices: 131 us -> none  [local(): lax.all_gather(local_weight, 'dp', axis=1, tiled=True)]
    pallas_call x0 -> x1, Pallas kernels: none -> 96.8 us  [local_part(): pl.pallas_call(kernel, out_shape=jax.ShapeDtypeStruct((ROWS, WIDTH), BF),...]
    all_to_all x3 -> x0, waiting for transfers between devices: 28.4 us -> none  [the longest x1 13 us: local(): lax.all_to_all(send_rows, 'dp', split_axis=0, concat_axis=0, tiled=True)]
    psum x1 -> x0, blocking collectives: 25.2 us -> none  [local(): lax.psum(partial_value.astype(jnp.bfloat16), 'tensor').astype(jnp.float32)]
    dot_general x3 -> x0, matrix products: 17.8 us -> none  [the longest x1 12.4 us: local(): jnp.dot(local_rows, lax.all_gather(local_weight, 'dp', axis=1, tiled=True...]
    all_to_all x3 -> x0, starting transfers between devices: 13.9 us -> none  [the longest x1 5.58 us: local(): lax.all_to_all(low_rank.reshape(rows_in.shape), 'dp', split_axis=0, conca...]
    ppermute x1 -> x0, starting transfers between devices: 8.6 us -> none  [shifted(): lax.ppermute(array, axis, [(i, (i + by) % count) for i in range(count)])]
    scatter x2 -> x0, local copies, waits for them, and re-layouts: 4.22 us -> none  [the longest x1 2.66 us: local(): send_rows = jnp.zeros((owner_count * capacity, feature_width), jnp.bfloat...]
  transfers between devices with their start and end apart: 6 -> 0, of which waited for: 5 -> 0; matrix products, arithmetic and copies ran while one was open for 5% -> 0% of each run, Pallas kernels for 0% -> 0%
where the time goes in v2:
time: 101 us; the launch traced here: 100 us
  Pallas kernels  96.8 us (96%)
  local copies, waits for them, and re-layouts  1.95 us (2%)
  other arithmetic  1.36 us (1%)
    pallas_call x1, Pallas kernels, local_part(): pl.pallas_call(kernel, out_shape=jax.ShapeDtypeStruct((ROWS, WIDTH), BF),...  96.8 us

profile of v2, /device:TPU:1, one launch (start us, length us, event | category | flops | bytes accessed | tf_op | source)
XLA Modules:
  0.0 100.1 jit_solution(3426017371682640859)
XLA Ops:
  0.0 0.1 pad.2.clone
  0.1 1.4 %add_add_fusion.ids_hbm = s32[8,256]{1,0:T(8,128)} fusion(s32[1,256]{1,0:T(1,128)} %param.11, s32[1,256]{1,0:T(1,128)} %bitcast.11, s32[8]{0:T(128)S(1)} %pad.2.clone), kind=kLoop, calls=%fused_computation | loop fusion | flops 4096 | bytes 10272 | tf_op jit(solution)/shard_map/concatenate | solution.py:405
  1.4 96.8 %shard_map.64 = bf16[256,1024]{1,0:T(8,128)(2,1)} custom-call(bf16[256,1024]{1,0:T(8,128)(2,1)} %bitcast.10, bf16[1024,512]{1,0:T(8,128)(2,1)} %bitcast.9, bf16[1024,1024]{1,0:T(8,128)(2,1)} %bitcast.7, bf16[1024,1024]{1,0:T(8,128)(2,1)} %bitcast.8, s32[8,256]{1,0:T(8,128)} %add_add_fusion.ids_hbm), custom_call_target="tpu_custom_call" | custom-call | tf_op jit(solution)/shard_map/pallas_call | solution.py:410
  98.3 1.9 %copy.8 = bf16[1,256,1024]{2,1,0:T(8,128)(2,1)} copy(bf16[1,256,1024]{2,1,0:T(8,128)(2,1)} %bitcast.6) | data formatting | bytes 1048576
  (1 shorter events, 0.0 us)

commit v3 on v2

--- a/solution.py
+++ b/solution.py
@@ -16,13 +16,15 @@
 GROUP = NY * CAP
 FLOWS = NQ * NY
 STEPS = 3
-LAGS = (0, 2, 5, 8, 10)
-ROUNDS = FLOWS + LAGS[4]
-SEND_W = {2: 2, 3: 6}
-PASS_W = {1: 1, 2: 5, 3: 9}
-ROUTE_AT = 9
-SHRINK_AT = (15, 15, 16, 16)
-EXPAND_AT = (19, 19, 20, 20)
+GAP = 1
+PERIOD = NY + GAP
+LAGS = (0, 2, 4, 6, 8)
+ROUNDS = NQ * PERIOD - GAP + LAGS[4]
+SEND_W = {2: 1, 3: 6}
+PASS_W = {1: 1, 2: 6, 3: 11}
+ROUTE_AT = 11
+SHRINK_AT = (17, 17, 18, 18)
+EXPAND_AT = (20, 21, 22, 23)
 PARTS = 4
 BF, F32 = jnp.bfloat16, jnp.float32
 
@@ -45,7 +47,7 @@
 
 def kernel(
     x_hbm, w_hbm, shrink_hbm, expand_hbm, ids_hbm, out_ref,
-    xg, wg, idg, rs, bt, xp, idp, aout, sout, ain, sin, shrink, expand, total, pin, spread, low, lin,
+    xg, wg, idg, rs, bt, xp, idp, aout, sout, ain, sin, shrink, expand, total, pin, spread, low, lin, acc,
     loc_sem, x_send, x_recv, id_send, id_recv, w_send, w_recv, p_send, p_recv, f_send, f_recv,
     g_send, g_recv, z_send, z_recv, r_send, r_recv, b_send, b_recv, rs_send, rs_recv,
 ):
@@ -73,8 +75,6 @@
     for q in range(NQ):
         load_w[q].start()
     load_id.start()
-    load_shrink.start()
-    load_expand.start()
 
     barrier = pltpu.get_barrier_semaphore()
     peers = [here((u + d) % NY, v, z) for d in range(1, NY)]
@@ -150,18 +150,21 @@
 
     load_x.wait()
     gx[0]()
-    for q in range(NQ):
-        load_w[q].wait()
-        if q not in SEND_W:
-            gw(q)[0]()
+    load_w[0].wait()
+    gw(0)[0]()
     load_id.wait()
     for d in range(1, NY):
         start(remote(idg.at[u], idg.at[u], id_send.at[d - 1], id_recv.at[d - 1], here((u + d) % NY, v, z)))
     start(remote(block_of(u), xp, p_send.at[0], p_recv.at[0], partner))
     start(remote(idg.at[u], idp, p_send.at[1], p_recv.at[1], partner))
 
+    load_shrink.start()
+    load_expand.start()
+    for q in range(1, NQ):
+        load_w[q].wait()
+    gw(0)[1]()
+    gw(1)[0]()
     gx[1]()
-    gw(0)[1]()
 
     upper = (
         lax.broadcasted_iota(jnp.int32, (ROWS, ROWS), 0) <= lax.broadcasted_iota(jnp.int32, (ROWS, ROWS), 1)
@@ -227,8 +230,11 @@
         rows = pl.ds(pl.multiple_of(row_block(f) * ROWS, ROWS), ROWS)
         return dot(xg[rows, :], wg[root // 2, f // NY], 1, 0)
 
-    def in_turn(f):
-        return (f >= 0) & (f < FLOWS)
+    def in_turn(i):
+        return (i >= 0) & (i < NQ * PERIOD) & (i % PERIOD < NY)
+
+    def flow(i):
+        return (i // PERIOD) * NY + i % PERIOD
 
     def first_direction(f):
         return f % 2
@@ -236,16 +242,18 @@
     def tile_step(i):
         @pl.when((odd == 0) & in_turn(i))
         def _():
-            part = product(i, (z + 4) % NZ).astype(BF)
+            f4 = flow(i)
+            part = product(f4, (z + 4) % NZ).astype(BF)
             for direction in range(2):
-                @pl.when(first_direction(i) == direction)
+                @pl.when(first_direction(f4) == direction)
                 def _():
-                    rs[direction, i, 0] = part
-                    ring_copy(i, direction, 0).start()
-
-        f3 = i - LAGS[1]
-
-        @pl.when((odd == 1) & in_turn(f3))
+                    rs[direction, f4, 0] = part
+                    ring_copy(f4, direction, 0).start()
+
+        i3 = i - LAGS[1]
+        f3 = flow(i3)
+
+        @pl.when((odd == 1) & in_turn(i3))
         def _():
             for direction in range(2):
                 root = (z + 3) % NZ if direction == 0 else (z + NZ - 3) % NZ
@@ -262,9 +270,10 @@
                 ring_copy(f3, direction, 0).start()
 
         away = 2 - odd
-        f1 = i - LAGS[2] - odd * (LAGS[3] - LAGS[2])
-
-        @pl.when(in_turn(f1))
+        i1 = i - LAGS[2] - odd * (LAGS[3] - LAGS[2])
+        f1 = flow(i1)
+
+        @pl.when(in_turn(i1))
         def _():
             for direction in range(2):
                 root = (z + away) % NZ if direction == 0 else (z + NZ - away) % NZ
@@ -272,9 +281,10 @@
                 rs[direction, f1, 1] = (part + arrived(f1, direction, 1)).astype(BF)
                 ring_copy(f1, direction, 1).start()
 
-        f0 = i - LAGS[4]
-
-        @pl.when((odd == 0) & in_turn(f0))
+        i0 = i - LAGS[4]
+        f0 = flow(i0)
+
+        @pl.when((odd == 0) & in_turn(i0))
         def _():
             part = product(f0, z)
             part = part + arrived(f0, 0, 2)
@@ -334,9 +344,9 @@
             return_copy(vv, b).start()
 
     def round_of(j, carry):
-        @pl.when(in_turn(j) & (j % NY == 0))
+        @pl.when(in_turn(j) & (j % PERIOD == 0))
         def _():
-            gw(j // NY)[5]()
+            gw(j // PERIOD)[5]()
 
         for f in range(1, NY):
             pl.when(j == f)(gx[1 + f])
@@ -362,24 +372,16 @@
     owner = idp[0:1, :]
     code = owner * CAP + arrivals(owner, upper)
     pick = (lax.broadcasted_iota(jnp.int32, (OWNERS * CAP, ROWS), 0) == code).astype(BF)
-    for o in range(OWNERS):
-        remote(lin.at[o], lin.at[o], r_send.at[0, 0], r_recv.at[o], partner).wait_recv()
-    got = lin[...].reshape(OWNERS * CAP, WIDTH)
-    for q in range(NQ):
-        for p in range(2):
-            remote(bt.at[p, q], bt.at[p, q], b_send.at[q], b_recv.at[p, q], partner).wait_recv()
-    for c in range(WIDTH // 256):
-        cols = slice(c * 256, (c + 1) * 256)
-        rows = dot(pick, got[:, cols], 0, 0)
-        p, q = (c * 256) // COLS, ((c * 256) % COLS) // CW
-        base = jnp.concatenate([bt[p, q + k] for k in range(256 // CW)], axis=1)
-        out_ref[:, cols] = (xp[:, cols].astype(F32) + base.astype(F32) + rows).astype(BF)
-
     for copy in started:
         copy.wait_send()
     gx[6]()
     for q in range(NQ):
         gw(q)[6]()
+    for d in range(1, NX):
+        route_copy(d, (v + d) % NX).wait_send()
+        slot_copy(d, (v + d) % NX).wait_send()
+    for d in range(1, NZ):
+        sum_copy(d).wait_send()
 
     def drain_flow(f, carry):
         for direction in range(2):
@@ -390,15 +392,23 @@
         pl.when(odd == 0)(lambda: last_copy(f).wait_send())
         return carry
 
-    lax.fori_loop(0, FLOWS, drain_flow, 0)
-    for d in range(1, NX):
-        route_copy(d, (v + d) % NX).wait_send()
-        slot_copy(d, (v + d) % NX).wait_send()
-    for d in range(1, NZ):
-        sum_copy(d).wait_send()
+    lax.fori_loop(0, FLOWS - NY, drain_flow, 0)
+
+    for o in range(OWNERS):
+        remote(lin.at[o], lin.at[o], r_send.at[0, 0], r_recv.at[o], partner).wait_recv()
+    for c in range(WIDTH // 256):
+        cols = slice(c * 256, (c + 1) * 256)
+        rows = dot(pick, lin[:, :, cols].reshape(OWNERS * CAP, 256), 0, 0)
+        acc[:, cols] = xp[:, cols].astype(F32) + rows
     for vv in range(NX):
         for b in range(NY):
             return_copy(vv, b).wait_send()
+    for q in range(NQ):
+        for p in range(2):
+            remote(bt.at[p, q], bt.at[p, q], b_send.at[q], b_recv.at[p, q], partner).wait_recv()
+            cols = slice(p * COLS + q * CW, p * COLS + (q + 1) * CW)
+            out_ref[:, cols] = (acc[:, cols] + bt[p, q].astype(F32)).astype(BF)
+    lax.fori_loop(FLOWS - NY, FLOWS, drain_flow, 0)
 
 
 def local_part(hidden_states, base_weight, shrink_weight, expand_weight, owner_ids, adapter_slots):
@@ -431,6 +441,7 @@
             pltpu.VMEM((SLOTS * RANK, GROUP), BF),
             pltpu.VMEM((NX, GROUP, WIDTH), BF),
             pltpu.VMEM((OWNERS, CAP, WIDTH), BF),
+            pltpu.VMEM((ROWS, WIDTH), F32),
             dma((4 + NQ,)),
             dma((6,)), dma((6,)),
             dma((NY - 1,)), dma((NY - 1,)),

time: 101 us -> 97.6 us (0.966)
  the two profiles are of different devices: /device:TPU:1 before, /device:TPU:31 now
where the time goes in v3:
time: 97.6 us; the launch traced here: 97.4 us
  Pallas kernels  94.1 us (96%)
  local copies, waits for them, and re-layouts  1.95 us (2%)
  other arithmetic  1.36 us (1%)
    pallas_call x1, Pallas kernels, local_part(): pl.pallas_call(kernel, out_shape=jax.ShapeDtypeStruct((ROWS, WIDTH), BF),...  94.1 us

profile of v3, /device:TPU:31, one launch (start us, length us, event | category | flops | bytes accessed | tf_op | source)
XLA Modules:
  0.0 97.4 jit_solution(446500013702964633)
XLA Ops:
  0.0 0.1 pad.2.clone
  0.1 1.4 %add_add_fusion.ids_hbm = s32[8,256]{1,0:T(8,128)} fusion(s32[1,256]{1,0:T(1,128)} %param.11, s32[1,256]{1,0:T(1,128)} %bitcast.11, s32[8]{0:T(128)S(1)} %pad.2.clone), kind=kLoop, calls=%fused_computation | loop fusion | flops 4096 | bytes 10272 | tf_op jit(solution)/shard_map/concatenate | solution.py:415
  1.4 94.1 %shard_map.64 = bf16[256,1024]{1,0:T(8,128)(2,1)} custom-call(bf16[256,1024]{1,0:T(8,128)(2,1)} %bitcast.10, bf16[1024,512]{1,0:T(8,128)(2,1)} %bitcast.9, bf16[1024,1024]{1,0:T(8,128)(2,1)} %bitcast.7, bf16[1024,1024]{1,0:T(8,128)(2,1)} %bitcast.8, s32[8,256]{1,0:T(8,128)} %add_add_fusion.ids_hbm), custom_call_target="tpu_custom_call" | custom-call | tf_op jit(solution)/shard_map/pallas_call | solution.py:420
  95.6 1.9 %copy.8 = bf16[1,256,1024]{2,1,0:T(8,128)(2,1)} copy(bf16[1,256,1024]{2,1,0:T(8,128)(2,1)} %bitcast.6) | data formatting | bytes 1048576
  (1 shorter events, 0.0 us)

commit v4 on v3

--- a/solution.py
+++ b/solution.py
@@ -155,8 +155,6 @@
     load_id.wait()
     for d in range(1, NY):
         start(remote(idg.at[u], idg.at[u], id_send.at[d - 1], id_recv.at[d - 1], here((u + d) % NY, v, z)))
-    start(remote(block_of(u), xp, p_send.at[0], p_recv.at[0], partner))
-    start(remote(idg.at[u], idp, p_send.at[1], p_recv.at[1], partner))
 
     load_shrink.start()
     load_expand.start()
@@ -165,6 +163,8 @@
     gw(0)[1]()
     gw(1)[0]()
     gx[1]()
+    start(remote(block_of(u), xp, p_send.at[0], p_recv.at[0], partner))
+    start(remote(idg.at[u], idp, p_send.at[1], p_recv.at[1], partner))
 
     upper = (
         lax.broadcasted_iota(jnp.int32, (ROWS, ROWS), 0) <= lax.broadcasted_iota(jnp.int32, (ROWS, ROWS), 1)
@@ -326,8 +326,9 @@
             low.at[vv, pl.ds(b * CAP, CAP), :], lin.at[dp], r_send.at[vv, b], r_recv.at[dp], there(b, vv, z)
         )
 
-    def expand_part(vv):
-        if vv == 0:
+    def expand_part(turn):
+        vv = (v + (2, 1, 3, 0)[turn]) % NX
+        if turn == 0:
             load_expand.wait()
             for d in range(1, NZ):
                 src = (z + NZ - d) % NZ
@@ -340,8 +341,8 @@
         for k in range(SLOTS):
             spread[k * RANK : (k + 1) * RANK, :] = jnp.where(slots == k, sums, 0.0).astype(BF)
         low[vv] = dot(spread[...], expand[...], 0, 0).astype(BF)
-        for b in range(NY):
-            return_copy(vv, b).start()
+        for d in (2, 1, 3, 0):
+            return_copy(vv, (u + d) % NY).start()
 
     def round_of(j, carry):
         @pl.when(in_turn(j) & (j % PERIOD == 0))

time: 97.6 us -> 95.1 us (0.974)
  the two profiles are of different devices: /device:TPU:31 before, /device:TPU:1 now
where the time goes in v4:
time: 95.1 us; the launch traced here: 94.6 us
  Pallas kernels  91.2 us (96%)
  local copies, waits for them, and re-layouts  1.95 us (2%)
  other arithmetic  1.36 us (1%)
    pallas_call x1, Pallas kernels, local_part(): pl.pallas_call(kernel, out_shape=jax.ShapeDtypeStruct((ROWS, WIDTH), BF),...  91.2 us

profile of v4, /device:TPU:1, one launch (start us, length us, event | category | flops | bytes accessed | tf_op | source)
XLA Modules:
  0.0 94.6 jit_solution(3780756581240253560)
XLA Ops:
  0.0 0.1 pad.2.clone
  0.1 1.4 %add_add_fusion.ids_hbm = s32[8,256]{1,0:T(8,128)} fusion(s32[1,256]{1,0:T(1,128)} %param.11, s32[1,256]{1,0:T(1,128)} %bitcast.11, s32[8]{0:T(128)S(1)} %pad.2.clone), kind=kLoop, calls=%fused_computation | loop fusion | flops 4096 | bytes 10272 | tf_op jit(solution)/shard_map/concatenate | solution.py:416
  1.4 91.2 %shard_map.64 = bf16[256,1024]{1,0:T(8,128)(2,1)} custom-call(bf16[256,1024]{1,0:T(8,128)(2,1)} %bitcast.10, bf16[1024,512]{1,0:T(8,128)(2,1)} %bitcast.9, bf16[1024,1024]{1,0:T(8,128)(2,1)} %bitcast.7, bf16[1024,1024]{1,0:T(8,128)(2,1)} %bitcast.8, s32[8,256]{1,0:T(8,128)} %add_add_fusion.ids_hbm), custom_call_target="tpu_custom_call" | custom-call | tf_op jit(solution)/shard_map/pallas_call | solution.py:421
  92.7 1.9 %copy.8 = bf16[1,256,1024]{2,1,0:T(8,128)(2,1)} copy(bf16[1,256,1024]{2,1,0:T(8,128)(2,1)} %bitcast.6) | data formatting | bytes 1048576
  (1 shorter events, 0.0 us)

commit v5 on v4

--- a/solution.py
+++ b/solution.py
@@ -190,7 +190,7 @@
             for vv in range(NX):
                 part = chosen[:, vv * GROUP : (vv + 1) * GROUP]
                 sout[vv] = part if b == 0 else sout[vv] + part
-        for d in range(1, NX):
+        for d in (2, 1, 3):
             to = (v + d) % NX
             route_copy(d, to).start()
             slot_copy(d, to).start()
@@ -315,7 +315,7 @@
 
         if c == PARTS - 1:
             pin[z] = total[...].astype(BF)
-            for d in range(1, NZ):
+            for d in (4, 3, 5, 2, 6, 1, 7):
                 sum_copy(d).start()
 
     def sum_copy(d):

time: 95.1 us -> 95.6 us (level)
  Pallas kernels: 91.2 us -> 92.2 us
where the time goes in v5:
time: 95.6 us; the launch traced here: 95.5 us
  Pallas kernels  92.2 us (96%)
  local copies, waits for them, and re-layouts  1.95 us (2%)
  other arithmetic  1.36 us (1%)
    pallas_call x1, Pallas kernels, local_part(): pl.pallas_call(kernel, out_shape=jax.ShapeDtypeStruct((ROWS, WIDTH), BF),...  92.2 us

profile of v5, /device:TPU:1, one launch (start us, length us, event | category | flops | bytes accessed | tf_op | source)
XLA Modules:
  0.0 95.5 jit_solution(6309302135131713577)
XLA Ops:
  0.0 0.1 pad.2.clone
  0.1 1.4 %add_add_fusion.ids_hbm = s32[8,256]{1,0:T(8,128)} fusion(s32[1,256]{1,0:T(1,128)} %param.11, s32[1,256]{1,0:T(1,128)} %bitcast.11, s32[8]{0:T(128)S(1)} %pad.2.clone), kind=kLoop, calls=%fused_computation | loop fusion | flops 4096 | bytes 10272 | tf_op jit(solution)/shard_map/concatenate | solution.py:416
  1.4 92.2 %shard_map.64 = bf16[256,1024]{1,0:T(8,128)(2,1)} custom-call(bf16[256,1024]{1,0:T(8,128)(2,1)} %bitcast.10, bf16[1024,512]{1,0:T(8,128)(2,1)} %bitcast.9, bf16[1024,1024]{1,0:T(8,128)(2,1)} %bitcast.7, bf16[1024,1024]{1,0:T(8,128)(2,1)} %bitcast.8, s32[8,256]{1,0:T(8,128)} %add_add_fusion.ids_hbm), custom_call_target="tpu_custom_call" | custom-call | tf_op jit(solution)/shard_map/pallas_call | solution.py:421
  93.6 1.9 %copy.8 = bf16[1,256,1024]{2,1,0:T(8,128)(2,1)} copy(bf16[1,256,1024]{2,1,0:T(8,128)(2,1)} %bitcast.6) | data formatting | bytes 1048576
  (1 shorter events, 0.0 us)
